TPU v7x, 32 devices: a whole 2x2x4 slice. The times are simulated.
32 devices in a mesh: expert: 8 (over z, y), dp: 4 (over x, core).
Axes of the slice: x: 2, y: 2, z: 4, core: 2. Of those that a mesh axis runs over, the one named last changes fastest.
Arguments:
- cotangent: bfloat16 [4096, 2048], P(('expert', 'dp')), may hold values from -4 to 4
- router_probs: bfloat16 [4096, 1], P(('expert', 'dp')), may hold values from 0.049804688 to 0.59765625
- slot_ids: int32 [4096, 1], P(('expert', 'dp')), may hold values from 0 to 7; in each aligned block of 128 rows (0 to 127, 128 to 255, ...) at most 24 rows name the same one
- saved_hidden: bfloat16 [8, 768, 1024], P('expert', 'dp'), may hold values from -6 to 6
- down_weight: bfloat16 [8, 2048, 512], P('expert', 'dp'), as said below
Outputs:
- grad_down: float32 [8, 2048, 512], P('expert', 'dp')
- grad_hidden: bfloat16 [8, 768, 1024], P('expert', 'dp')
- grad_probs: float32 [4096, 1], P(('expert', 'dp'))
Inputs may be any that keep to these rules, and one draw needn't show every extreme that they name: `slot_ids`: in the 128 tokens of one device, each token names one slot, no slot is named by more than 24 tokens, a bound that some block reaches. `down_weight`: slots s and s + 4 hold the same expert's weights.
All inputs are finite; a program needn't handle non-finite values.
Results may differ from a plain program's by a relative error of at most 0.007.
Values may be sent and summed in bfloat16 or wider, within the bound.
A program may use at most 64 MiB of HBM per device.

v0:
```python
import jax
import jax.numpy as jnp
from jax import lax
from jax.sharding import PartitionSpec as P


def from_partner(block, axis, bit):
    count = lax.axis_size(axis)
    route = []
    for low in range(count):
        high = low | 1 << bit
        if high != low and high < count:
            route += [(low, high), (high, low)]
    return lax.ppermute(block, axis, route)


def on_device(cotangent, router_probs, slot_ids, saved_hidden, down_weight):
    expert_count = lax.axis_size("expert")
    tok_count, pick_count = slot_ids.shape
    model_width = cotangent.shape[1]
    capacity = 3 * tok_count * pick_count // (2 * expert_count)
    flat_slot = slot_ids.reshape(-1)
    slot_hits = (flat_slot[:, None] == jnp.arange(expert_count, dtype=jnp.int32)[None, :]).astype(
        jnp.int32
    )
    earlier = jnp.cumsum(slot_hits, axis=0) - slot_hits
    position = jnp.sum(earlier * slot_hits, axis=1)
    target = flat_slot * capacity + position
    places = (
        target[:, None] == jnp.arange(expert_count * capacity, dtype=jnp.int32)[None, :]
    ).astype(jnp.float32)
    places = places.reshape(tok_count, pick_count, expert_count * capacity)
    spread = jnp.sum(places, axis=1).astype(jnp.bfloat16)
    sent_rows = lax.dot_general(
        spread, cotangent, (((0,), (0,)), ((), ())), preferred_element_type=jnp.float32
    ).astype(jnp.bfloat16)
    sent_probs = jnp.einsum("tkr,tk->r", places, router_probs.astype(jnp.float32)).astype(
        jnp.bfloat16
    )
    rows_in, probs_in = (
        lax.all_to_all(
            sent_rows.reshape(expert_count, capacity, model_width),
            "expert",
            split_axis=0,
            concat_axis=1,
            tiled=True,
        ),
        lax.all_to_all(
            sent_probs.reshape(expert_count, capacity),
            "expert",
            split_axis=0,
            concat_axis=1,
            tiled=True,
        ),
    )
    cot_rows = rows_in[0]
    prob_rows = probs_in[0]
    hidden = saved_hidden[0]
    hidden_width = hidden.shape[1] // 2
    gate_pre = hidden[:, :hidden_width].astype(jnp.float32)
    up_pre = hidden[:, hidden_width:].astype(jnp.float32)
    gate_sig = jax.nn.sigmoid(gate_pre)
    gate_act = gate_pre * gate_sig
    activation = (gate_act * up_pre).astype(jnp.bfloat16)
    scaled = (prob_rows.astype(jnp.float32)[:, None] * cot_rows.astype(jnp.float32)).astype(
        jnp.bfloat16
    )
    weight_piece = lax.all_gather(down_weight, "dp", axis=1, tiled=True)[0]
    out_part = lax.dot_general(
        activation, weight_piece, (((1,), (1,)), ((), ())), preferred_element_type=jnp.float32
    )
    cot_part = cot_rows.astype(jnp.float32)
    prob_grad = jnp.sum(cot_part * out_part, axis=1)
    grad_act = jnp.dot(scaled, weight_piece, preferred_element_type=jnp.float32)
    grad_act, prob_grad = (grad_act, prob_grad)
    grad_gate = grad_act * up_pre * gate_sig * (1.0 + gate_pre * (1.0 - gate_sig))
    grad_up = grad_act * gate_act
    grad_hidden = jnp.concatenate([grad_gate, grad_up], axis=1).astype(jnp.bfloat16)[None]
    prob_back = lax.all_to_all(
        prob_grad[None, :], "expert", split_axis=1, concat_axis=0, tiled=True
    )
    grad_probs = jnp.einsum("tkr,r->tk", places, prob_back.reshape(-1))
    columns = lax.all_to_all(scaled, "dp", split_axis=1, concat_axis=0, tiled=True)
    weight_grad = lax.dot_general(
        columns,
        lax.all_gather(activation, "dp", axis=0, tiled=True),
        (((0,), (0,)), ((), ())),
        preferred_element_type=jnp.float32,
    )
    partner = from_partner(
        weight_grad.astype(jnp.bfloat16), "expert", expert_count.bit_length() - 2
    ).astype(weight_grad.dtype)
    grad_down = (weight_grad + partner)[None]
    return (grad_down, grad_hidden, grad_probs)


def solution(mesh):
    placed = (
        P(("expert", "dp"), None),
        P(("expert", "dp"), None),
        P(("expert", "dp"), None),
        P("expert", "dp", None),
        P("expert", "dp", None),
    )
    return jax.shard_map(
        on_device,
        mesh=mesh,
        in_specs=placed,
        out_specs=(P("expert", "dp", None), P("expert", "dp", None), P(("expert", "dp"), None)),
        check_vma=False,
    )
```

profile of v0, /device:TPU:1, one launch (start us, length us, event | category | flops | bytes accessed | tf_op | source)
XLA Modules:
  0.0 112.0 jit_solution(1497874289278578347)
XLA Ops:
  7.2 0.0 copy-start
  7.2 0.0 all-gather.2.cloned.1.call-start
  7.2 0.7 all-gather.2.cloned.1.call-update
  7.9 0.7 fusion.21
  8.7 0.2 reduce_window_sum.11
  8.8 0.8 select_reduce_fusion
  9.7 0.7 fusion.24
  10.3 0.8 fusion.18
  11.1 0.7 all_to_all.47
  11.8 6.4 %all-to-all-start = ((bf16[8,1,24]{2,1,0:T(2,128)(2,1)}), bf16[8,1,24]{2,1,0:T(2,128)(2,1)S(1)}, u32[]{:S(2)}, u32[]{:S(2)}) async-start(bf16[8,1,24]{2,1,0:T(2,128)(2,1)} %all_to_all.47), calls=%async_computation | async-start | bytes 8192 | tf_op jit(solution)/shard_map/all_to_all | solution.py:48
  18.2 0.0 copy-done
  18.2 1.3 %convolution_convert_fusion = bf16[192,2048]{1,0:T(8,128)(2,1)} fusion(bf16[128,2048]{1,0:T(8,128)(2,1)S(1)} %copy-done, s32[128]{0:T(128)S(1)} %fusion.24), kind=kOutput, calls=%fused_computation.1 | convolution fusion | flops 101130240 | bytes 1311232 | tf_op jit(solution)/shard_map/dot_general | solution.py:34
  19.6 3.9 %all-to-all-done = bf16[8,1,24]{2,1,0:T(2,128)(2,1)S(1)} async-done(((bf16[8,1,24]{2,1,0:T(2,128)(2,1)}), bf16[8,1,24]{2,1,0:T(2,128)(2,1)S(1)}, u32[]{:S(2)}, u32[]{:S(2)}) %all-to-all-start) | async-done | bytes 416 | tf_op jit(solution)/shard_map/all_to_all | solution.py:48
  23.5 3.5 %all-to-all-start.1 = ((bf16[8,24,2048]{2,1,0:T(8,128)(2,1)}), bf16[8,24,2048]{2,1,0:T(8,128)(2,1)S(1)}, u32[]{:S(2)}, u32[]{:S(2)}) async-start(bf16[8,24,2048]{2,1,0:T(8,128)(2,1)} %bitcast.6), calls=%async_computation.1 | async-start | bytes 1572864 | tf_op jit(solution)/shard_map/all_to_all | solution.py:41
  27.0 0.1 reshape.178
  27.1 18.2 %all-to-all-done.1 = bf16[8,24,2048]{2,1,0:T(8,128)(2,1)S(1)} async-done(((bf16[8,24,2048]{2,1,0:T(8,128)(2,1)}), bf16[8,24,2048]{2,1,0:T(8,128)(2,1)S(1)}, u32[]{:S(2)}, u32[]{:S(2)}) %all-to-all-start.1) | async-done | bytes 786464 | tf_op jit(solution)/shard_map/all_to_all | solution.py:41
  45.3 1.2 %reshape.179 = f32[192,4,512]{2,1,0:T(4,128)S(1)} reshape(bf16[8,24,2048]{2,1,0:T(8,128)(2,1)S(1)} %all-to-all-done.1) | data formatting | bytes 2359296 | tf_op jit(solution)/shard_map/convert_element_type | solution.py:65
  46.6 0.3 multiply_convert_fusion.1
  46.9 1.0 copy.11
  47.9 7.0 %all-to-all-start.2 = ((bf16[192,4,512]{2,0,1:T(8,128)(2,1)}), bf16[192,4,512]{2,0,1:T(8,128)(2,1)}, u32[]{:S(2)}, u32[]{:S(2)}) async-start(bf16[192,4,512]{2,0,1:T(8,128)(2,1)} %copy.11), calls=%async_computation.2 | async-start | bytes 1572864 | tf_op jit(solution)/shard_map/all_to_all | solution.py:83
  54.9 0.2 convert_element_type.107
  55.1 1.1 multiply_convert_fusion
  56.2 0.0 all-gather.2.cloned.1.call-done
  56.2 3.2 %fusion.15 = (bf16[1,192,512]{2,1,0:T(8,128)(2,1)S(1)}, bf16[1,192,512]{2,1,0:T(8,128)(2,1)}, bf16[192,512]{1,0:T(8,128)(2,1)S(1)}) fusion(bf16[192,1024]{1,0:T(8,128)(2,1)} %bitcast.52, bf16[192,2048]{1,0:T(8,128)(2,1)} %bitcast.48, bf16[1,2048,512]{2,1,0:T(8,128)(2,1)} %all-gather.2.cloned.1.call-done), kind=kOutput, calls=%fused_computation.26 | convolution fusion | flops 404324352 | bytes 3866624 | tf_op jit(solution)/shard_map/dot_general | solution.py:74
  59.4 12.6 %all_gather.6 = bf16[768,512]{1,0:T(8,128)(2,1)} all-gather(bf16[192,512]{1,0:T(8,128)(2,1)S(1)} %get-tuple-element.5), channel_id=1, replica_groups=mesh['expert'=8,'dp'=4] {'dp'}, dimensions={0}, use_global_device_ids=true | all-gather | bytes 983040 | tf_op jit(solution)/shard_map/all_gather | solution.py:86
  72.0 0.0 all-to-all-done.2
  72.0 0.0 copy-start.1
  72.0 2.9 %fusion.25 = (bf16[512,512]{1,0:T(8,128)(2,1)}, f32[512,512]{1,0:T(8,128)S(1)}) fusion(bf16[768,512]{1,0:T(8,128)(2,1)} %bitcast.8, bf16[768,512]{1,0:T(8,128)(2,1)} %all_gather.6), kind=kOutput, calls=%fused_computation.41 | convolution fusion | flops 402915328 | bytes 3145728 | tf_op jit(solution)/shard_map/dot_general | solution.py:84
  74.9 0.0 collective-permute-start
  74.9 0.0 copy-done.1
  74.9 0.9 fusion.3
  75.8 0.7 all_to_all.45
  76.5 4.4 %all-to-all-start.3 = ((f32[1,8,24]{2,0,1:T(1,128)}), f32[1,8,24]{2,0,1:T(1,128)S(1)}, u32[]{:S(2)}, u32[]{:S(2)}) async-start(f32[1,8,24]{2,0,1:T(1,128)} %all_to_all.45), calls=%async_computation.3 | async-start | bytes 8192 | tf_op jit(solution)/shard_map/all_to_all | solution.py:79
  80.9 1.7 %pad_maximum_fusion = bf16[1,192,1024]{2,1,0:T(8,128)(2,1)} fusion(bf16[1,192,512]{2,1,0:T(8,128)(2,1)} %get-tuple-element.4, bf16[1,192,512]{2,1,0:T(8,128)(2,1)S(1)} %get-tuple-element.3), kind=kLoop, calls=%fused_computation.23 | loop fusion | flops 786432 | bytes 786432 | tf_op jit(solution)/shard_map/concatenate | solution.py:78
  82.6 18.4 %all-to-all-done.3 = f32[1,8,24]{2,0,1:T(1,128)S(1)} async-done(((f32[1,8,24]{2,0,1:T(1,128)}), f32[1,8,24]{2,0,1:T(1,128)S(1)}, u32[]{:S(2)}, u32[]{:S(2)}) %all-to-all-start.3) | async-done | bytes 800 | tf_op jit(solution)/shard_map/all_to_all | solution.py:79
  101.0 0.5 broadcast.59
  101.5 0.7 reduce.7
  102.2 0.1 reshape.184
  102.3 0.7 convolution_bitcast_fusion
  102.9 0.0 collective-permute-done
  102.9 2.2 %add_bitcast_fusion = f32[1,512,512]{2,1,0:T(8,128)} fusion(f32[512,512]{1,0:T(8,128)S(1)} %get-tuple-element.7, bf16[512,512]{1,0:T(8,128)(2,1)} %collective-permute-done), kind=kLoop, calls=%fused_computation.9 | loop fusion | flops 524288 | bytes 2621440 | tf_op jit(solution)/shard_map/broadcast_in_dim | solution.py:93
  (3 shorter events, 0.0 us)
Async XLA Ops:
  7.2 11.1 %copy-start = (bf16[128,2048]{1,0:T(8,128)(2,1)S(1)}, bf16[128,2048]{1,0:T(8,128)(2,1)}, u32[]{:S(2)}) copy-start(bf16[128,2048]{1,0:T(8,128)(2,1)} %param.5) | copy-start | bytes 1572868
  7.2 49.0 %all-gather.2.cloned.1.call-start = ((), (), s32[]{:S(2)}) async-start(), calls=%async_computation.4 | async-start | bytes 2621440 | tf_op jit(solution)/shard_map/all_gather | solution.py:68
  11.8 11.6 %all-to-all-start = ((bf16[8,1,24]{2,1,0:T(2,128)(2,1)}), bf16[8,1,24]{2,1,0:T(2,128)(2,1)S(1)}, u32[]{:S(2)}, u32[]{:S(2)}) async-start(bf16[8,1,24]{2,1,0:T(2,128)(2,1)} %all_to_all.47), calls=%async_computation | async-start | bytes 8192 | tf_op jit(solution)/shard_map/all_to_all | solution.py:48
  23.5 21.9 %all-to-all-start.1 = ((bf16[8,24,2048]{2,1,0:T(8,128)(2,1)}), bf16[8,24,2048]{2,1,0:T(8,128)(2,1)S(1)}, u32[]{:S(2)}, u32[]{:S(2)}) async-start(bf16[8,24,2048]{2,1,0:T(8,128)(2,1)} %bitcast.6), calls=%async_computation.1 | async-start | bytes 1572864 | tf_op jit(solution)/shard_map/all_to_all | solution.py:41
  47.9 24.0 %all-to-all-start.2 = ((bf16[192,4,512]{2,0,1:T(8,128)(2,1)}), bf16[192,4,512]{2,0,1:T(8,128)(2,1)}, u32[]{:S(2)}, u32[]{:S(2)}) async-start(bf16[192,4,512]{2,0,1:T(8,128)(2,1)} %copy.11), calls=%async_computation.2 | async-start | bytes 1572864 | tf_op jit(solution)/shard_map/all_to_all | solution.py:83
  72.0 2.9 %copy-start.1 = (bf16[1,2048,512]{2,1,0:T(8,128)(2,1)S(1)}, bf16[1,2048,512]{2,1,0:T(8,128)(2,1)}, u32[]{:S(2)}) copy-start(bf16[1,2048,512]{2,1,0:T(8,128)(2,1)} %all-gather.2.cloned.1.call-done) | copy-start | bytes 6291460
  74.9 28.0 %collective-permute-start = (bf16[512,512]{1,0:T(8,128)(2,1)}, bf16[512,512]{1,0:T(8,128)(2,1)}, u32[]{:S(2)}, u32[]{:S(2)}) collective-permute-start(bf16[512,512]{1,0:T(8,128)(2,1)} %get-tuple-element.6), channel_id=1, source_target_pairs={{0,16},{16,0},{4,20},{20,4},{8,24},{24,8},{12,28},{28,12},{1,17},{... | collective-permute-start | bytes 1572872 | tf_op jit(solution)/shard_map/ppermute | solution.py:14
  76.5 24.5 %all-to-all-start.3 = ((f32[1,8,24]{2,0,1:T(1,128)}), f32[1,8,24]{2,0,1:T(1,128)S(1)}, u32[]{:S(2)}, u32[]{:S(2)}) async-start(f32[1,8,24]{2,0,1:T(1,128)} %all_to_all.45), calls=%async_computation.3 | async-start | bytes 8192 | tf_op jit(solution)/shard_map/all_to_all | solution.py:79
Sparse Core Ops, SparseCore 0:
  9.6 25.0 all-gather.1
where the time goes:
time: 113 us; the launch traced here: 112 us
  waiting for transfers between devices  41.1 us (36%)
  starting transfers between devices  21.4 us (19%)
  between operations  14.1 us (12%)
  blocking collectives  12.6 us (11%)
  matrix products  9.85 us (9%)
  other arithmetic  8.56 us (8%)
  local copies, waits for them, and re-layouts  4.36 us (4%)
    all_to_all x1, waiting for transfers between devices, on_device(): lax.all_to_all(prob_grad[None, :], 'expert', split_axis=1, concat_axis=0,...  18.4 us
    all_to_all x1, waiting for transfers between devices, on_device(): lax.all_to_all(sent_rows.reshape(expert_count, capacity, model_width), 'e...  18.2 us
    all_gather x1, blocking collectives, on_device(): lax.all_gather(activation, 'dp', axis=0, tiled=True)  12.6 us
    all_to_all x1, starting transfers between devices, on_device(): lax.all_to_all(scaled, 'dp', split_axis=1, concat_axis=0, tiled=True)  6.99 us
    all_to_all x1, starting transfers between devices, on_device(): lax.all_to_all(sent_probs.reshape(expert_count, capacity), 'expert', spli...  6.38 us
    all_to_all x1, starting transfers between devices, on_device(): lax.all_to_all(prob_grad[None, :], 'expert', split_axis=1, concat_axis=0,...  4.4 us
    all_to_all x1, waiting for transfers between devices, on_device(): lax.all_to_all(sent_probs.reshape(expert_count, capacity), 'expert', spli...  3.9 us
    all_to_all x1, starting transfers between devices, on_device(): lax.all_to_all(sent_rows.reshape(expert_count, capacity, model_width), 'e...  3.55 us
  transfers between devices with their start and end apart: 6, of which 3 were waited for; matrix products, arithmetic and copies ran while one was open for 15% of the time, Pallas kernels for 0%

commit v1 on v0

v1 whole, which is shorter than its diff:
```python
import functools

import jax
import jax.numpy as jnp
import numpy as np
from jax import lax
from jax.experimental import pallas as pl
from jax.experimental.pallas import tpu as pltpu
from jax.sharding import PartitionSpec as P

MESH = pl.DeviceIdType.MESH
F32 = jnp.float32
BF16 = jnp.bfloat16


def kernel(
    E, N, C, cot_ref, prob_ref, slot_ref, hid_ref, w_ref, by_dp_ref, by_e_ref,
    down_ref, hidden_ref, probs_ref,
    send1, got1, act, act_rows, send2, rows, gsend, gpart, psend, ppart, pg, scaled, spread,
    s1s, s1r, as_, ar, s2s, s2r, gs, gr, ps, pr, qs, qr,
):
    e, d = lax.axis_index("expert"), lax.axis_index("dp")
    tok, width = cot_ref.shape
    block = width // N
    ff = act.shape[2]
    NC, EC = N * C, E * C
    half = lax.rem(e + E // 2, E)

    def copy(src, dst, ss, rs, where):
        return pltpu.make_async_remote_copy(
            src_ref=src, dst_ref=dst, send_sem=ss, recv_sem=rs, device_id=where, device_id_type=MESH
        )

    def peers(n, me, body):
        def step(k, carry):
            body(lax.rem(me + k, n))
            return carry

        lax.fori_loop(1, n, step, 0)

    barrier = pltpu.get_barrier_semaphore()
    peers(N, d, lambda j: pl.semaphore_signal(barrier, inc=1, device_id=(e, j), device_id_type=MESH))
    peers(E, e, lambda j: pl.semaphore_signal(barrier, inc=1, device_id=(j, d), device_id_type=MESH))

    slot = slot_ref[...]
    lanes = lax.broadcasted_iota(jnp.int32, (tok, 128), 1)
    hits = jnp.where(lanes == slot, 1.0, 0.0).astype(F32)
    row_i = lax.broadcasted_iota(jnp.int32, (tok, tok), 0)
    col_i = lax.broadcasted_iota(jnp.int32, (tok, tok), 1)
    before = jnp.where(col_i < row_i, 1.0, 0.0).astype(BF16)
    earlier = jnp.dot(before, hits.astype(BF16), preferred_element_type=F32)
    position = jnp.sum(earlier * hits, axis=1, keepdims=True)
    target = slot.astype(F32) * C + position
    target_row = jnp.sum(jnp.where(row_i == col_i, target, 0.0), axis=0, keepdims=True)
    spread[...] = jnp.where(
        lax.broadcasted_iota(jnp.int32, (EC, tok), 0).astype(F32) == target_row, 1.0, 0.0
    ).astype(BF16)
    prob = prob_ref[...].astype(F32)
    scaled[...] = (cot_ref[...].astype(F32) * prob).astype(BF16)

    def piece(j):
        cols = pl.ds(pl.multiple_of(j * block, block), block)
        return jnp.dot(spread[...], scaled[:, cols], preferred_element_type=F32).astype(BF16)

    pl.semaphore_wait(barrier, N - 1 + E - 1)

    def one(j):
        send1[j] = piece(j)
        copy(send1.at[j], got1.at[d], s1s.at[j], s1r.at[d], (e, j)).start()

    peers(N, d, one)
    got1[d] = piece(d)

    gate = hid_ref[:, :ff].astype(F32)
    up = hid_ref[:, ff:].astype(F32)
    act[d] = (gate * jax.nn.sigmoid(gate) * up).astype(BF16)
    peers(N, d, lambda j: copy(act.at[d], act.at[d], as_.at[j], ar.at[d], (e, j)).start())
    peers(N, d, lambda j: copy(send1.at[j], got1.at[j], s1s.at[j], s1r.at[j], (e, j)).wait_recv())

    lane_r = lax.broadcasted_iota(jnp.int32, (NC, N * EC), 1)

    def pick(j):
        return jnp.where(lane_r == by_dp_ref[...] + j * C, 1.0, 0.0).astype(BF16)

    def select(j, ref):
        whole = ref[...].reshape(N * EC, ref.shape[2])
        return jnp.dot(pick(j), whole, preferred_element_type=F32).astype(BF16)

    def two(j):
        send2[j] = select(j, got1)
        copy(send2.at[j], rows.at[e], s2s.at[j], s2r.at[e], (j, d)).start()

    peers(E, e, two)
    rows[e] = select(e, got1)

    peers(N, d, lambda j: copy(act.at[d], act.at[j], as_.at[j], ar.at[j], (e, j)).wait_recv())

    def order(j, carry):
        act_rows[j] = select(j, act)
        return carry

    lax.fori_loop(0, E, order, 0)
    peers(E, e, lambda j: copy(send2.at[j], rows.at[j], s2s.at[j], s2r.at[j], (j, d)).wait_recv())

    parts = psend.shape[0]
    step = block // parts
    lined = act_rows[...].reshape(E * NC, ff)
    for c in range(parts):
        left = rows[:, :, c * step : (c + 1) * step].reshape(E * NC, step)
        grad = lax.dot_general(left, lined, (((0,), (0,)), ((), ())), preferred_element_type=F32)
        down_ref[c * step : (c + 1) * step, :] = grad
        psend[c] = grad.astype(BF16)
        copy(psend.at[c], ppart.at[c], ps.at[c], pr.at[c], (half, d)).start()

    lane_g = lax.broadcasted_iota(jnp.int32, (EC, E * NC), 1)

    def share(j):
        mine = jnp.where(lane_g == by_e_ref[...] + j * C, 1.0, 0.0).astype(BF16)
        ordered = jnp.dot(mine, rows[...].reshape(E * NC, block), preferred_element_type=F32)
        return jnp.dot(ordered.astype(BF16), w_ref[...], preferred_element_type=F32)

    def three(j):
        gsend[j] = share(j).astype(BF16)
        copy(gsend.at[j], gpart.at[d], gs.at[j], gr.at[d], (e, j)).start()

    peers(N, d, three)
    total = share(d)
    peers(N, d, lambda j: copy(gsend.at[j], gpart.at[j], gs.at[j], gr.at[j], (e, j)).wait_recv())
    total = lax.fori_loop(
        1, N, lambda k, t: t + gpart[lax.rem(d + k, N)].astype(F32), total
    )
    gate = hid_ref[:, :ff].astype(F32)
    up = hid_ref[:, ff:].astype(F32)
    sig = jax.nn.sigmoid(gate)
    pg_col = jnp.sum(total * act[d].astype(F32), axis=1, keepdims=True)
    eye = lax.broadcasted_iota(jnp.int32, (EC, EC), 0) == lax.broadcasted_iota(jnp.int32, (EC, EC), 1)
    pg_row = jnp.sum(jnp.where(eye, pg_col, 0.0), axis=0, keepdims=True)
    pg[e] = jnp.broadcast_to(pg_row, (8, EC))
    peers(E, e, lambda j: copy(pg.at[e], pg.at[e], qs.at[j], qr.at[e], (j, d)).start())
    hidden_ref[:, :ff] = (total * up * sig * (1.0 + gate * (1.0 - sig))).astype(BF16)
    hidden_ref[:, ff:] = (total * gate * sig).astype(BF16)

    peers(E, e, lambda j: copy(pg.at[e], pg.at[j], qs.at[j], qr.at[j], (j, d)).wait_recv())
    place = position + (e * C).astype(F32)
    found = lax.broadcasted_iota(jnp.int32, (tok, EC), 1).astype(F32) == place
    probs_ref[...] = (
        lax.fori_loop(
            0,
            E,
            lambda s, t: t
            + jnp.sum(jnp.where(found & (slot == s), pg[s][0:1, :], 0.0), axis=1, keepdims=True),
            jnp.zeros((tok, 1), F32),
        )
        / prob
    )

    for c in range(parts):
        copy(psend.at[c], ppart.at[c], ps.at[c], pr.at[c], (half, d)).wait_recv()
        down_ref[c * step : (c + 1) * step, :] += ppart[c].astype(F32)

    def sent_dp(j):
        copy(send1.at[j], got1.at[d], s1s.at[j], s1r.at[d], (e, j)).wait_send()
        copy(act.at[d], act.at[d], as_.at[j], ar.at[d], (e, j)).wait_send()
        copy(gsend.at[j], gpart.at[d], gs.at[j], gr.at[d], (e, j)).wait_send()

    def sent_e(j):
        copy(send2.at[j], rows.at[e], s2s.at[j], s2r.at[e], (j, d)).wait_send()
        copy(pg.at[e], pg.at[e], qs.at[j], qr.at[e], (j, d)).wait_send()

    peers(N, d, sent_dp)
    peers(E, e, sent_e)
    for c in range(parts):
        copy(psend.at[c], ppart.at[c], ps.at[c], pr.at[c], (half, d)).wait_send()


def on_device(E, N, cotangent, router_probs, slot_ids, saved_hidden, down_weight):
    tok, width = cotangent.shape
    C = 3 * tok // (2 * E)
    NC, EC = N * C, E * C
    block, ff = down_weight.shape[1:]
    parts = max(1, block // 256)
    by_dp = np.array([[j // C * EC + j % C] for j in range(NC)], np.int32)
    by_e = np.array([[i // C * NC + i % C] for i in range(EC)], np.int32)
    dma = pltpu.SemaphoreType.DMA
    vmem = pl.BlockSpec(memory_space=pltpu.VMEM)
    down, hidden, probs = pl.pallas_call(
        functools.partial(kernel, E, N, C),
        out_shape=(
            jax.ShapeDtypeStruct((block, ff), F32),
            jax.ShapeDtypeStruct((EC, 2 * ff), BF16),
            jax.ShapeDtypeStruct((tok, 1), F32),
        ),
        in_specs=[vmem] * 7,
        out_specs=(vmem,) * 3,
        scratch_shapes=[
            pltpu.VMEM((N, EC, block), BF16),
            pltpu.VMEM((N, EC, block), BF16),
            pltpu.VMEM((N, EC, ff), BF16),
            pltpu.VMEM((E, NC, ff), BF16),
            pltpu.VMEM((E, NC, block), BF16),
            pltpu.VMEM((E, NC, block), BF16),
            pltpu.VMEM((N, EC, ff), BF16),
            pltpu.VMEM((N, EC, ff), BF16),
            pltpu.VMEM((parts, block // parts, ff), BF16),
            pltpu.VMEM((parts, block // parts, ff), BF16),
            pltpu.VMEM((E, 8, EC), F32),
            pltpu.VMEM((tok, width), BF16),
            pltpu.VMEM((EC, tok), BF16),
            dma((N,)), dma((N,)), dma((N,)), dma((N,)), dma((E,)), dma((E,)),
            dma((N,)), dma((N,)), dma((parts,)), dma((parts,)), dma((E,)), dma((E,)),
        ],
        compiler_params=pltpu.CompilerParams(
            collective_id=0, has_side_effects=True, vmem_limit_bytes=56 * 2**20
        ),
        name="expert_backward",
    )(cotangent, router_probs, slot_ids, saved_hidden[0], down_weight[0], by_dp, by_e)
    return down[None], hidden[None], probs


def solution(mesh):
    placed = (
        P(("expert", "dp"), None),
        P(("expert", "dp"), None),
        P(("expert", "dp"), None),
        P("expert", "dp", None),
        P("expert", "dp", None),
    )
    return jax.shard_map(
        functools.partial(on_device, mesh.shape["expert"], mesh.shape["dp"]),
        mesh=mesh,
        in_specs=placed,
        out_specs=(P("expert", "dp", None), P("expert", "dp", None), P(("expert", "dp"), None)),
        check_vma=False,
    )
```

time: 113 us -> 74.8 us (0.66)
  Pallas kernels: 0 us -> 67.3 us
  waiting for transfers between devices: 41.1 us -> 0 us
  starting transfers between devices: 21.4 us -> 0 us
  between operations: 14.1 us -> 0.65 us
  blocking collectives: 12.6 us -> 0 us
  matrix products: 9.85 us -> 0 us
  other arithmetic: 8.56 us -> 0 us
  local copies, waits for them, and re-layouts: 4.36 us -> 6.61 us
    pallas_call x0 -> x1, Pallas kernels: none -> 67.3 us  [on_device(): pl.pallas_call(functools.partial(kernel, E, N, C), out_shape=(jax.ShapeDt...]
    all_to_all x4 -> x0, waiting for transfers between devices: 40.5 us -> none  [the longest x1 18.4 us: on_device(): lax.all_to_all(prob_grad[None, :], 'expert', split_axis=1, concat_axis=0,...]
    all_to_all x4 -> x0, starting transfers between devices: 21.3 us -> none  [the longest x1 6.99 us: on_device(): lax.all_to_all(scaled, 'dp', split_axis=1, concat_axis=0, tiled=True)]
    all_gather x1 -> x0, blocking collectives: 12.6 us -> none  [on_device(): lax.all_gather(activation, 'dp', axis=0, tiled=True)]
    dot_general x6 -> x0, matrix products: 9.85 us -> none  [the longest x1 3.21 us: on_device(): grad_act = jnp.dot(scaled, weight_piece, preferred_element_type=jnp.float32)]
    unnamed x4 -> x11, local copies, waits for them, and re-layouts: 0.01 us -> 6.61 us
    convert_element_type x7 -> x0, other arithmetic: 2.36 us -> none  [the longest x2 1.42 us: on_device(): (prob_rows.astype(jnp.float32)[:, None] * cot_rows.astype(jnp.float32)).a...]
    convert_element_type x3 -> x0, local copies, waits for them, and re-layouts: 2.34 us -> none  [the longest x1 1.24 us: on_device(): cot_rows.astype(jnp.float32)]
  transfers between devices with their start and end apart: 6 -> 0, of which waited for: 3 -> 0; matrix products, arithmetic and copies ran while one was open for 15% -> 0% of each run, Pallas kernels for 0% -> 0%
where the time goes in v1:
time: 74.8 us; the launch traced here: 74.6 us
  Pallas kernels  67.3 us (90%)
  local copies, waits for them, and re-layouts  6.61 us (9%)
    pallas_call x1, Pallas kernels, on_device(): pl.pallas_call(functools.partial(kernel, E, N, C), out_shape=(jax.ShapeDt...  67.3 us
    unnamed x11, local copies, waits for them, and re-layouts  6.61 us

profile of v1, /device:TPU:1, one launch (start us, length us, event | category | flops | bytes accessed | tf_op | source)
XLA Modules:
  0.0 74.6 jit_solution(8092792577342187166)
XLA Ops:
  0.6 0.0 copy-start.1
  0.6 0.6 copy-done.1
  1.3 0.0 copy-start.2
  1.3 0.7 copy.10.prob_ref
  2.0 0.0 copy-done.2
  2.0 0.7 copy.11.slot_ref
  2.8 67.3 %expert_backward.1 = (f32[512,512]{1,0:T(8,128)}, bf16[192,1024]{1,0:T(8,128)(2,1)}, f32[128,1]{1,0:T(8,128)}) custom-call(bf16[128,2048]{1,0:T(8,128)(2,1)} %cot_ref.1, bf16[128,1]{1,0:T(8,128)(2,1)} %copy.10.prob_ref, s32[128,1]{1,0:T(8,128)} %copy.11.slot_ref, bf16[192,1024]{1,0:T(8,128)(2,1)} %bitcast.7, bf16[512,512]{1,0:T(8,128)(2,1)} %bitcast.5, ...), custom_call_target="tpu_custom_call" | custom-call | tf_op jit(solution)/shard_map/expert_backward/pallas_call | solution.py:186
  70.1 1.4 %copy.12 = f32[128,1]{0,1:T(1,128)} copy(f32[128,1]{1,0:T(8,128)} %get-tuple-element.11) | data formatting | bytes 1024
  71.5 0.0 copy-start
  71.5 2.3 %copy.15 = f32[1,512,512]{2,1,0:T(8,128)} copy(f32[1,512,512]{2,1,0:T(8,128)} %bitcast.4) | data formatting | bytes 2097152
  73.8 0.0 copy-done
  73.8 0.7 copy.16
Async XLA Ops:
  0.6 0.7 copy-start.1
  1.3 0.7 copy-start.2
  71.5 2.3 %copy-start = (bf16[192,1024]{1,0:T(8,128)(2,1)S(1)}, bf16[192,1024]{1,0:T(8,128)(2,1)}, u32[]{:S(2)}) copy-start(bf16[192,1024]{1,0:T(8,128)(2,1)} %get-tuple-element.7) | copy-start | bytes 1179652

commit v2 on v1

v2 whole, which is shorter than its diff:
```python
import functools

import jax
import jax.numpy as jnp
import numpy as np
from jax import lax
from jax.experimental import pallas as pl
from jax.experimental.pallas import tpu as pltpu
from jax.sharding import PartitionSpec as P

MESH = pl.DeviceIdType.MESH
F32 = jnp.float32
BF16 = jnp.bfloat16


def kernel(
    E, N, C, cot_ref, prob_ref, slot_ref, hid_ref, w_ref, by_dp_ref, by_act_ref, by_e_ref,
    down_ref, hidden_ref, probs_ref,
    send1, got1, act, act_rows, send2, rows, gsend, gpart, psend, ppart, pg, scaled, spread,
    xact, xsend, xpart, s1s, s1r, as_, ar, s2s, s2r, gs, gr, ps, pr, qs, qr, xs, xr,
):
    e, d = lax.axis_index("expert"), lax.axis_index("dp")
    tok, width = cot_ref.shape
    block = width // N
    ff = act.shape[3]
    H = E // 2
    NC, EC, HC = N * C, E * C, H * C
    mine, x = lax.div(e, H), lax.rem(e, H)
    other = lax.rem(e + H, E)
    start = mine * H

    def copy(src, dst, ss, rs, where):
        return pltpu.make_async_remote_copy(
            src_ref=src, dst_ref=dst, send_sem=ss, recv_sem=rs, device_id=where, device_id_type=MESH
        )

    def peers(n, me, body):
        def step(k, carry):
            body(lax.rem(me + k, n))
            return carry

        lax.fori_loop(1, n, step, 0)

    barrier = pltpu.get_barrier_semaphore()
    peers(N, d, lambda j: pl.semaphore_signal(barrier, inc=1, device_id=(e, j), device_id_type=MESH))
    peers(
        H, x,
        lambda j: pl.semaphore_signal(barrier, inc=1, device_id=(start + j, d), device_id_type=MESH),
    )
    pl.semaphore_signal(barrier, inc=1, device_id=(other, d), device_id_type=MESH)

    def half_rows(g):
        return pl.ds(pl.multiple_of(g * HC, HC), HC)

    def activation(g):
        gate = hid_ref[half_rows(g), :ff].astype(F32)
        up = hid_ref[half_rows(g), ff:].astype(F32)
        return (gate * jax.nn.sigmoid(gate) * up).astype(BF16)

    xact[...] = activation(1 - mine)

    slot = slot_ref[...]
    lanes = lax.broadcasted_iota(jnp.int32, (tok, 128), 1)
    hits = jnp.where(lanes == slot, 1.0, 0.0).astype(F32)
    row_i = lax.broadcasted_iota(jnp.int32, (tok, tok), 0)
    col_i = lax.broadcasted_iota(jnp.int32, (tok, tok), 1)
    before = jnp.where(col_i < row_i, 1.0, 0.0).astype(BF16)
    earlier = jnp.dot(before, hits.astype(BF16), preferred_element_type=F32)
    position = jnp.sum(earlier * hits, axis=1, keepdims=True)
    target = slot.astype(F32) * C + position
    target_row = jnp.sum(jnp.where(row_i == col_i, target, 0.0), axis=0, keepdims=True)
    spread[...] = jnp.where(
        lax.broadcasted_iota(jnp.int32, (EC, tok), 0).astype(F32) == target_row, 1.0, 0.0
    ).astype(BF16)
    prob = prob_ref[...].astype(F32)
    scaled[...] = (cot_ref[...].astype(F32) * prob).astype(BF16)

    def piece(j):
        cols = pl.ds(pl.multiple_of(j * block, block), block)
        return jnp.dot(spread[...], scaled[:, cols], preferred_element_type=F32).astype(BF16)

    pl.semaphore_wait(barrier, N - 1 + H)
    cross_act = copy(xact, act.at[1, d], xs.at[0], xr.at[0], (other, d))
    cross_act.start()

    def one(j):
        send1[j] = piece(j)
        copy(send1.at[j], got1.at[d], s1s.at[j], s1r.at[d], (e, j)).start()

    peers(N, d, one)
    got1[d] = piece(d)

    act[0, d] = activation(mine)

    def give(i):
        peers(N, d, lambda j: copy(act.at[i, d], act.at[i, d], as_.at[i, j], ar.at[i, d], (e, j)).start())

    give(0)
    peers(N, d, lambda j: copy(send1.at[j], got1.at[j], s1s.at[j], s1r.at[j], (e, j)).wait_recv())

    lane_r = lax.broadcasted_iota(jnp.int32, (NC, N * EC), 1)

    def select(base, ref):
        pick = jnp.where(lane_r == base, 1.0, 0.0).astype(BF16)
        whole = ref[...].reshape(N * EC, ref.shape[-1])
        return jnp.dot(pick, whole, preferred_element_type=F32).astype(BF16)

    def rows_of(s):
        return select(by_dp_ref[...] + s * C, got1)

    def two(j):
        send2[j, 0] = rows_of(start + j)
        send2[j, 1] = rows_of((1 - mine) * H + j)
        copy(send2.at[j], rows.at[x], s2s.at[j], s2r.at[x], (start + j, d)).start()

    peers(H, x, two)
    cross_act.wait_recv()
    give(1)
    rows[x, 0] = rows_of(e)
    rows[x, 1] = rows_of(other)

    for i in range(2):
        peers(
            N, d,
            lambda j: copy(act.at[i, d], act.at[i, j], as_.at[i, j], ar.at[i, j], (e, j)).wait_recv(),
        )

    def order(j, carry):
        for i in range(2):
            act_rows[j, i] = select(by_act_ref[...] + (i * N * HC + j * C), act)
        return carry

    lax.fori_loop(0, H, order, 0)
    peers(
        H, x,
        lambda j: copy(send2.at[j], rows.at[j], s2s.at[j], s2r.at[j], (start + j, d)).wait_recv(),
    )

    parts = psend.shape[0]
    step = block // parts
    lined = act_rows[...].reshape(E * NC, ff)
    for c in range(parts):
        left = rows[:, :, :, c * step : (c + 1) * step].reshape(E * NC, step)
        grad = lax.dot_general(left, lined, (((0,), (0,)), ((), ())), preferred_element_type=F32)
        down_ref[c * step : (c + 1) * step, :] = grad
        psend[c] = grad.astype(BF16)
        copy(psend.at[c], ppart.at[c], ps.at[c], pr.at[c], (other, d)).start()

    lane_g = lax.broadcasted_iota(jnp.int32, (EC, E * NC), 1)

    def share(j):
        pick = jnp.where(lane_g == by_e_ref[...] + j * C, 1.0, 0.0).astype(BF16)
        ordered = jnp.dot(pick, rows[...].reshape(E * NC, block), preferred_element_type=F32)
        return jnp.dot(ordered.astype(BF16), w_ref[...], preferred_element_type=F32)

    def three(j):
        gsend[j] = share(j).astype(BF16)
        copy(gsend.at[j], gpart.at[d], gs.at[j], gr.at[d], (e, j)).start()

    peers(N, d, three)
    total = share(d)
    peers(N, d, lambda j: copy(gsend.at[j], gpart.at[j], gs.at[j], gr.at[j], (e, j)).wait_recv())
    total = lax.fori_loop(
        1, N, lambda k, t: t + gpart[lax.rem(d + k, N)].astype(F32), total
    )
    xsend[...] = total[HC:].astype(BF16)
    cross_grad = copy(xsend, xpart, xs.at[1], xr.at[1], (other, d))
    cross_grad.start()
    own_act = jnp.concatenate([act[0, d].astype(F32), act[1, d].astype(F32)], axis=0)
    pg_col = jnp.sum(total * own_act, axis=1, keepdims=True)
    eye = lax.broadcasted_iota(jnp.int32, (EC, EC), 0) == lax.broadcasted_iota(jnp.int32, (EC, EC), 1)
    pg_row = jnp.sum(jnp.where(eye, pg_col, 0.0), axis=0, keepdims=True)
    pg[x] = jnp.broadcast_to(pg_row, (8, EC))
    peers(H, x, lambda j: copy(pg.at[x], pg.at[x], qs.at[j], qr.at[x], (start + j, d)).start())

    def finish(g, grad):
        gate = hid_ref[half_rows(g), :ff].astype(F32)
        up = hid_ref[half_rows(g), ff:].astype(F32)
        sig = jax.nn.sigmoid(gate)
        hidden_ref[half_rows(g), :ff] = (grad * up * sig * (1.0 + gate * (1.0 - sig))).astype(BF16)
        hidden_ref[half_rows(g), ff:] = (grad * gate * sig).astype(BF16)

    finish(mine, total[:HC])

    peers(H, x, lambda j: copy(pg.at[x], pg.at[j], qs.at[j], qr.at[j], (start + j, d)).wait_recv())
    upper = jnp.where(slot >= H, 1, 0)
    away = jnp.where(upper == mine, 0, 1)
    expert = slot - upper * H
    place = position + (away * HC + x * C).astype(F32)
    found = lax.broadcasted_iota(jnp.int32, (tok, EC), 1).astype(F32) == place
    probs_ref[...] = (
        lax.fori_loop(
            0,
            H,
            lambda j, t: t
            + jnp.sum(jnp.where(found & (expert == j), pg[j][0:1, :], 0.0), axis=1, keepdims=True),
            jnp.zeros((tok, 1), F32),
        )
        / prob
    )
    cross_grad.wait_recv()
    finish(1 - mine, xpart[...].astype(F32))

    for c in range(parts):
        copy(psend.at[c], ppart.at[c], ps.at[c], pr.at[c], (other, d)).wait_recv()
        down_ref[c * step : (c + 1) * step, :] += ppart[c].astype(F32)

    def sent_dp(j):
        copy(send1.at[j], got1.at[d], s1s.at[j], s1r.at[d], (e, j)).wait_send()
        for i in range(2):
            copy(act.at[i, d], act.at[i, d], as_.at[i, j], ar.at[i, d], (e, j)).wait_send()
        copy(gsend.at[j], gpart.at[d], gs.at[j], gr.at[d], (e, j)).wait_send()

    def sent_e(j):
        copy(send2.at[j], rows.at[x], s2s.at[j], s2r.at[x], (start + j, d)).wait_send()
        copy(pg.at[x], pg.at[x], qs.at[j], qr.at[x], (start + j, d)).wait_send()

    peers(N, d, sent_dp)
    peers(H, x, sent_e)
    cross_act.wait_send()
    cross_grad.wait_send()
    for c in range(parts):
        copy(psend.at[c], ppart.at[c], ps.at[c], pr.at[c], (other, d)).wait_send()


def on_device(E, N, cotangent, router_probs, slot_ids, saved_hidden, down_weight):
    tok, width = cotangent.shape
    C = 3 * tok // (2 * E)
    H = E // 2
    NC, EC, HC = N * C, E * C, H * C
    block, ff = down_weight.shape[1:]
    parts = max(1, block // 256)
    by_dp = np.array([[j // C * EC + j % C] for j in range(NC)], np.int32)
    by_act = np.array([[j // C * HC + j % C] for j in range(NC)], np.int32)
    by_e = np.array(
        [[i // C % H * 2 * NC + i // HC * NC + i % C] for i in range(EC)], np.int32
    )
    dma = pltpu.SemaphoreType.DMA
    vmem = pl.BlockSpec(memory_space=pltpu.VMEM)
    down, hidden, probs = pl.pallas_call(
        functools.partial(kernel, E, N, C),
        out_shape=(
            jax.ShapeDtypeStruct((block, ff), F32),
            jax.ShapeDtypeStruct((EC, 2 * ff), BF16),
            jax.ShapeDtypeStruct((tok, 1), F32),
        ),
        in_specs=[vmem] * 8,
        out_specs=(vmem,) * 3,
        scratch_shapes=[
            pltpu.VMEM((N, EC, block), BF16),
            pltpu.VMEM((N, EC, block), BF16),
            pltpu.VMEM((2, N, HC, ff), BF16),
            pltpu.VMEM((H, 2, NC, ff), BF16),
            pltpu.VMEM((H, 2, NC, block), BF16),
            pltpu.VMEM((H, 2, NC, block), BF16),
            pltpu.VMEM((N, EC, ff), BF16),
            pltpu.VMEM((N, EC, ff), BF16),
            pltpu.VMEM((parts, block // parts, ff), BF16),
            pltpu.VMEM((parts, block // parts, ff), BF16),
            pltpu.VMEM((H, 8, EC), F32),
            pltpu.VMEM((tok, width), BF16),
            pltpu.VMEM((EC, tok), BF16),
            pltpu.VMEM((HC, ff), BF16),
            pltpu.VMEM((HC, ff), BF16),
            pltpu.VMEM((HC, ff), BF16),
            dma((N,)), dma((N,)), dma((2, N)), dma((2, N)), dma((H,)), dma((H,)),
            dma((N,)), dma((N,)), dma((parts,)), dma((parts,)), dma((H,)), dma((H,)),
            dma((2,)), dma((2,)),
        ],
        compiler_params=pltpu.CompilerParams(
            collective_id=0, has_side_effects=True, vmem_limit_bytes=56 * 2**20
        ),
        name="expert_backward",
    )(cotangent, router_probs, slot_ids, saved_hidden[0], down_weight[0], by_dp, by_act, by_e)
    return down[None], hidden[None], probs


def solution(mesh):
    placed = (
        P(("expert", "dp"), None),
        P(("expert", "dp"), None),
        P(("expert", "dp"), None),
        P("expert", "dp", None),
        P("expert", "dp", None),
    )
    return jax.shard_map(
        functools.partial(on_device, mesh.shape["expert"], mesh.shape["dp"]),
        mesh=mesh,
        in_specs=placed,
        out_specs=(P("expert", "dp", None), P("expert", "dp", None), P(("expert", "dp"), None)),
        check_vma=False,
    )
```

time: 74.8 us -> 64.5 us (0.86)
  Pallas kernels: 67.3 us -> 56.7 us
    pallas_call x1, Pallas kernels: 67.3 us -> 56.7 us  [on_device(): pl.pallas_call(functools.partial(kernel, E, N, C), out_shape=(jax.ShapeDt...]
where the time goes in v2:
time: 64.5 us; the launch traced here: 63.9 us
  Pallas kernels  56.7 us (88%)
  local copies, waits for them, and re-layouts  6.61 us (10%)
  between operations  0.65 us (1%)
    pallas_call x1, Pallas kernels, on_device(): pl.pallas_call(functools.partial(kernel, E, N, C), out_shape=(jax.ShapeDt...  56.7 us
    unnamed x11, local copies, waits for them, and re-layouts  6.61 us

profile of v2, /device:TPU:1, one launch (start us, length us, event | category | flops | bytes accessed | tf_op | source)
XLA Modules:
  0.0 63.9 jit_solution(17220682964638051548)
XLA Ops:
  0.6 0.0 copy-start.1
  0.6 0.6 %copy-done.1 = bf16[128,1]{0,1:T(2,128)(2,1)S(1)} copy-done((bf16[128,1]{0,1:T(2,128)(2,1)S(1)}, bf16[128,1]{0,1:T(2,128)(2,1)}, u32[]{:S(2)}) %copy-start.1) | copy-done | bytes 280
  1.3 0.0 copy-start.2
  1.3 0.7 %copy.11.prob_ref = bf16[128,1]{1,0:T(8,128)(2,1)} copy(bf16[128,1]{0,1:T(2,128)(2,1)S(1)} %copy-done.1) | data formatting | bytes 512 | tf_op args[1]
  2.0 0.0 copy-done.2
  2.0 0.7 %copy.12.slot_ref = s32[128,1]{1,0:T(8,128)} copy(s32[128,1]{0,1:T(1,128)S(1)} %copy-done.2) | data formatting | bytes 1024 | tf_op args[2]
  2.8 56.7 %expert_backward.1 = (f32[512,512]{1,0:T(8,128)}, bf16[192,1024]{1,0:T(8,128)(2,1)}, f32[128,1]{1,0:T(8,128)}) custom-call(bf16[128,2048]{1,0:T(8,128)(2,1)} %cot_ref.1, bf16[128,1]{1,0:T(8,128)(2,1)} %copy.11.prob_ref, s32[128,1]{1,0:T(8,128)} %copy.12.slot_ref, bf16[192,1024]{1,0:T(8,128)(2,1)} %bitcast.7, bf16[512,512]{1,0:T(8,128)(2,1)} %bitcast.5, ...), custom_call_target="tpu_custom_call" | custom-call | tf_op jit(solution)/shard_map/expert_backward/pallas_call | solution.py:240
  59.4 1.4 %copy.13 = f32[128,1]{0,1:T(1,128)} copy(f32[128,1]{1,0:T(8,128)} %get-tuple-element.11) | data formatting | bytes 1024
  60.9 0.0 copy-start
  60.9 2.3 %copy.16 = f32[1,512,512]{2,1,0:T(8,128)} copy(f32[1,512,512]{2,1,0:T(8,128)} %bitcast.4) | data formatting | bytes 2097152
  63.2 0.0 copy-done
  63.2 0.7 %copy.17 = bf16[1,192,1024]{2,1,0:T(8,128)(2,1)} copy(bf16[1,192,1024]{2,1,0:T(8,128)(2,1)S(1)} %bitcast.6) | data formatting | bytes 786432
Async XLA Ops:
  0.6 0.7 %copy-start.1 = (bf16[128,1]{0,1:T(2,128)(2,1)S(1)}, bf16[128,1]{0,1:T(2,128)(2,1)}, u32[]{:S(2)}) copy-start(bf16[128,1]{0,1:T(2,128)(2,1)} %param.9) | copy-start | bytes 772
  1.3 0.7 %copy-start.2 = (s32[128,1]{0,1:T(1,128)S(1)}, s32[128,1]{0,1:T(1,128)}, u32[]{:S(2)}) copy-start(s32[128,1]{0,1:T(1,128)} %param.10) | copy-start | bytes 1540
  60.9 2.3 %copy-start = (bf16[192,1024]{1,0:T(8,128)(2,1)S(1)}, bf16[192,1024]{1,0:T(8,128)(2,1)}, u32[]{:S(2)}) copy-start(bf16[192,1024]{1,0:T(8,128)(2,1)} %get-tuple-element.7) | copy-start | bytes 1179652

commit v3 on v2

--- a/solution.py
+++ b/solution.py
@@ -75,20 +75,25 @@
     prob = prob_ref[...].astype(F32)
     scaled[...] = (cot_ref[...].astype(F32) * prob).astype(BF16)
 
-    def piece(j):
-        cols = pl.ds(pl.multiple_of(j * block, block), block)
+    parts = psend.shape[0]
+    step = block // parts
+
+    def piece(j, c):
+        cols = pl.ds(pl.multiple_of(j * block + c * step, step), step)
         return jnp.dot(spread[...], scaled[:, cols], preferred_element_type=F32).astype(BF16)
 
     pl.semaphore_wait(barrier, N - 1 + H)
     cross_act = copy(xact, act.at[1, d], xs.at[0], xr.at[0], (other, d))
     cross_act.start()
 
-    def one(j):
-        send1[j] = piece(j)
-        copy(send1.at[j], got1.at[d], s1s.at[j], s1r.at[d], (e, j)).start()
-
-    peers(N, d, one)
-    got1[d] = piece(d)
+    for c in range(parts):
+
+        def one(j):
+            send1[c, j] = piece(j, c)
+            copy(send1.at[c, j], got1.at[c, d], s1s.at[c, j], s1r.at[c, d], (e, j)).start()
+
+        peers(N, d, one)
+        got1[c, d] = piece(d, c)
 
     act[0, d] = activation(mine)
 
@@ -96,28 +101,36 @@
         peers(N, d, lambda j: copy(act.at[i, d], act.at[i, d], as_.at[i, j], ar.at[i, d], (e, j)).start())
 
     give(0)
-    peers(N, d, lambda j: copy(send1.at[j], got1.at[j], s1s.at[j], s1r.at[j], (e, j)).wait_recv())
-
     lane_r = lax.broadcasted_iota(jnp.int32, (NC, N * EC), 1)
 
     def select(base, ref):
         pick = jnp.where(lane_r == base, 1.0, 0.0).astype(BF16)
-        whole = ref[...].reshape(N * EC, ref.shape[-1])
-        return jnp.dot(pick, whole, preferred_element_type=F32).astype(BF16)
-
-    def rows_of(s):
-        return select(by_dp_ref[...] + s * C, got1)
-
-    def two(j):
-        send2[j, 0] = rows_of(start + j)
-        send2[j, 1] = rows_of((1 - mine) * H + j)
-        copy(send2.at[j], rows.at[x], s2s.at[j], s2r.at[x], (start + j, d)).start()
-
-    peers(H, x, two)
-    cross_act.wait_recv()
-    give(1)
-    rows[x, 0] = rows_of(e)
-    rows[x, 1] = rows_of(other)
+        return jnp.dot(pick, ref.reshape(N * EC, ref.shape[-1]), preferred_element_type=F32).astype(BF16)
+
+    def rows_of(s, c):
+        return select(by_dp_ref[...] + s * C, got1[c])
+
+    for c in range(parts):
+        peers(
+            N, d,
+            lambda j: copy(
+                send1.at[c, j], got1.at[c, j], s1s.at[c, j], s1r.at[c, j], (e, j)
+            ).wait_recv(),
+        )
+
+        def two(j):
+            send2[c, j, 0] = rows_of(start + j, c)
+            send2[c, j, 1] = rows_of((1 - mine) * H + j, c)
+            copy(
+                send2.at[c, j], rows.at[c, x], s2s.at[c, j], s2r.at[c, x], (start + j, d)
+            ).start()
+
+        peers(H, x, two)
+        rows[c, x, 0] = rows_of(e, c)
+        rows[c, x, 1] = rows_of(other, c)
+        if c == 0:
+            cross_act.wait_recv()
+            give(1)
 
     for i in range(2):
         peers(
@@ -127,20 +140,19 @@
 
     def order(j, carry):
         for i in range(2):
-            act_rows[j, i] = select(by_act_ref[...] + (i * N * HC + j * C), act)
+            act_rows[j, i] = select(by_act_ref[...] + (i * N * HC + j * C), act[...])
         return carry
 
     lax.fori_loop(0, H, order, 0)
-    peers(
-        H, x,
-        lambda j: copy(send2.at[j], rows.at[j], s2s.at[j], s2r.at[j], (start + j, d)).wait_recv(),
-    )
-
-    parts = psend.shape[0]
-    step = block // parts
     lined = act_rows[...].reshape(E * NC, ff)
     for c in range(parts):
-        left = rows[:, :, :, c * step : (c + 1) * step].reshape(E * NC, step)
+        peers(
+            H, x,
+            lambda j: copy(
+                send2.at[c, j], rows.at[c, j], s2s.at[c, j], s2r.at[c, j], (start + j, d)
+            ).wait_recv(),
+        )
+        left = rows[c].reshape(E * NC, step)
         grad = lax.dot_general(left, lined, (((0,), (0,)), ((), ())), preferred_element_type=F32)
         down_ref[c * step : (c + 1) * step, :] = grad
         psend[c] = grad.astype(BF16)
@@ -150,8 +162,13 @@
 
     def share(j):
         pick = jnp.where(lane_g == by_e_ref[...] + j * C, 1.0, 0.0).astype(BF16)
-        ordered = jnp.dot(pick, rows[...].reshape(E * NC, block), preferred_element_type=F32)
-        return jnp.dot(ordered.astype(BF16), w_ref[...], preferred_element_type=F32)
+        part = jnp.zeros((EC, ff), F32)
+        for c in range(parts):
+            ordered = jnp.dot(pick, rows[c].reshape(E * NC, step), preferred_element_type=F32)
+            part += jnp.dot(
+                ordered.astype(BF16), w_ref[c * step : (c + 1) * step, :], preferred_element_type=F32
+            )
+        return part
 
     def three(j):
         gsend[j] = share(j).astype(BF16)
@@ -206,13 +223,17 @@
         down_ref[c * step : (c + 1) * step, :] += ppart[c].astype(F32)
 
     def sent_dp(j):
-        copy(send1.at[j], got1.at[d], s1s.at[j], s1r.at[d], (e, j)).wait_send()
+        for c in range(parts):
+            copy(send1.at[c, j], got1.at[c, d], s1s.at[c, j], s1r.at[c, d], (e, j)).wait_send()
         for i in range(2):
             copy(act.at[i, d], act.at[i, d], as_.at[i, j], ar.at[i, d], (e, j)).wait_send()
         copy(gsend.at[j], gpart.at[d], gs.at[j], gr.at[d], (e, j)).wait_send()
 
     def sent_e(j):
-        copy(send2.at[j], rows.at[x], s2s.at[j], s2r.at[x], (start + j, d)).wait_send()
+        for c in range(parts):
+            copy(
+                send2.at[c, j], rows.at[c, x], s2s.at[c, j], s2r.at[c, x], (start + j, d)
+            ).wait_send()
         copy(pg.at[x], pg.at[x], qs.at[j], qr.at[x], (start + j, d)).wait_send()
 
     peers(N, d, sent_dp)
@@ -247,12 +268,12 @@
         in_specs=[vmem] * 8,
         out_specs=(vmem,) * 3,
         scratch_shapes=[
-            pltpu.VMEM((N, EC, block), BF16),
-            pltpu.VMEM((N, EC, block), BF16),
+            pltpu.VMEM((parts, N, EC, block // parts), BF16),
+            pltpu.VMEM((parts, N, EC, block // parts), BF16),
             pltpu.VMEM((2, N, HC, ff), BF16),
             pltpu.VMEM((H, 2, NC, ff), BF16),
-            pltpu.VMEM((H, 2, NC, block), BF16),
-            pltpu.VMEM((H, 2, NC, block), BF16),
+            pltpu.VMEM((parts, H, 2, NC, block // parts), BF16),
+            pltpu.VMEM((parts, H, 2, NC, block // parts), BF16),
             pltpu.VMEM((N, EC, ff), BF16),
             pltpu.VMEM((N, EC, ff), BF16),
             pltpu.VMEM((parts, block // parts, ff), BF16),
@@ -263,7 +284,7 @@
             pltpu.VMEM((HC, ff), BF16),
             pltpu.VMEM((HC, ff), BF16),
             pltpu.VMEM((HC, ff), BF16),
-            dma((N,)), dma((N,)), dma((2, N)), dma((2, N)), dma((H,)), dma((H,)),
+            dma((parts, N)), dma((parts, N)), dma((2, N)), dma((2, N)), dma((parts, H)), dma((parts, H)),
             dma((N,)), dma((N,)), dma((parts,)), dma((parts,)), dma((H,)), dma((H,)),
             dma((2,)), dma((2,)),
         ],

time: 64.5 us -> 65.8 us (1.020)
  Pallas kernels: 56.7 us -> 58 us
    pallas_call x1, Pallas kernels: 56.7 us -> 58 us  [on_device(): pl.pallas_call(functools.partial(kernel, E, N, C), out_shape=(jax.ShapeDt...]
where the time goes in v3:
time: 65.8 us; the launch traced here: 65.2 us
  Pallas kernels  58 us (88%)
  local copies, waits for them, and re-layouts  6.61 us (10%)
    pallas_call x1, Pallas kernels, on_device(): pl.pallas_call(functools.partial(kernel, E, N, C), out_shape=(jax.ShapeDt...  58 us
    unnamed x11, local copies, waits for them, and re-layouts  6.61 us

profile of v3, /device:TPU:1, one launch (start us, length us, event | category | flops | bytes accessed | tf_op | source)
XLA Modules:
  0.0 65.2 jit_solution(13314120659972335495)
XLA Ops:
  0.6 0.0 copy-start.1
  0.6 0.6 copy-done.1
  1.3 0.0 copy-start.2
  1.3 0.7 %copy.11.prob_ref = bf16[128,1]{1,0:T(8,128)(2,1)} copy(bf16[128,1]{0,1:T(2,128)(2,1)S(1)} %copy-done.1) | data formatting | bytes 512 | tf_op args[1]
  2.0 0.0 copy-done.2
  2.0 0.7 %copy.12.slot_ref = s32[128,1]{1,0:T(8,128)} copy(s32[128,1]{0,1:T(1,128)S(1)} %copy-done.2) | data formatting | bytes 1024 | tf_op args[2]
  2.8 58.0 %expert_backward.1 = (f32[512,512]{1,0:T(8,128)}, bf16[192,1024]{1,0:T(8,128)(2,1)}, f32[128,1]{1,0:T(8,128)}) custom-call(bf16[128,2048]{1,0:T(8,128)(2,1)} %cot_ref.1, bf16[128,1]{1,0:T(8,128)(2,1)} %copy.11.prob_ref, s32[128,1]{1,0:T(8,128)} %copy.12.slot_ref, bf16[192,1024]{1,0:T(8,128)(2,1)} %bitcast.7, bf16[512,512]{1,0:T(8,128)(2,1)} %bitcast.5, ...), custom_call_target="tpu_custom_call" | custom-call | tf_op jit(solution)/shard_map/expert_backward/pallas_call | solution.py:261
  60.7 1.4 %copy.13 = f32[128,1]{0,1:T(1,128)} copy(f32[128,1]{1,0:T(8,128)} %get-tuple-element.11) | data formatting | bytes 1024
  62.2 0.0 copy-start
  62.2 2.3 %copy.16 = f32[1,512,512]{2,1,0:T(8,128)} copy(f32[1,512,512]{2,1,0:T(8,128)} %bitcast.4) | data formatting | bytes 2097152
  64.5 0.0 copy-done
  64.5 0.7 %copy.17 = bf16[1,192,1024]{2,1,0:T(8,128)(2,1)} copy(bf16[1,192,1024]{2,1,0:T(8,128)(2,1)S(1)} %bitcast.6) | data formatting | bytes 786432
Async XLA Ops:
  0.6 0.7 %copy-start.1 = (bf16[128,1]{0,1:T(2,128)(2,1)S(1)}, bf16[128,1]{0,1:T(2,128)(2,1)}, u32[]{:S(2)}) copy-start(bf16[128,1]{0,1:T(2,128)(2,1)} %param.9) | copy-start | bytes 772
  1.3 0.7 %copy-start.2 = (s32[128,1]{0,1:T(1,128)S(1)}, s32[128,1]{0,1:T(1,128)}, u32[]{:S(2)}) copy-start(s32[128,1]{0,1:T(1,128)} %param.10) | copy-start | bytes 1540
  62.2 2.3 %copy-start = (bf16[192,1024]{1,0:T(8,128)(2,1)S(1)}, bf16[192,1024]{1,0:T(8,128)(2,1)}, u32[]{:S(2)}) copy-start(bf16[192,1024]{1,0:T(8,128)(2,1)} %get-tuple-element.7) | copy-start | bytes 1179652

commit v4 on v2

--- a/solution.py
+++ b/solution.py
@@ -39,7 +39,7 @@
             body(lax.rem(me + k, n))
             return carry
 
-        lax.fori_loop(1, n, step, 0)
+        lax.fori_loop(1, n, step, 0, unroll=n <= 8)
 
     barrier = pltpu.get_barrier_semaphore()
     peers(N, d, lambda j: pl.semaphore_signal(barrier, inc=1, device_id=(e, j), device_id_type=MESH))
@@ -98,26 +98,27 @@
     give(0)
     peers(N, d, lambda j: copy(send1.at[j], got1.at[j], s1s.at[j], s1r.at[j], (e, j)).wait_recv())
 
-    lane_r = lax.broadcasted_iota(jnp.int32, (NC, N * EC), 1)
+    lane_r = lax.broadcasted_iota(jnp.int32, (2 * NC, N * EC), 1)
+    second = lax.broadcasted_iota(jnp.int32, (2 * NC, 1), 0) >= NC
 
     def select(base, ref):
         pick = jnp.where(lane_r == base, 1.0, 0.0).astype(BF16)
         whole = ref[...].reshape(N * EC, ref.shape[-1])
-        return jnp.dot(pick, whole, preferred_element_type=F32).astype(BF16)
-
-    def rows_of(s):
-        return select(by_dp_ref[...] + s * C, got1)
+        picked = jnp.dot(pick, whole, preferred_element_type=F32).astype(BF16)
+        return picked.reshape(2, NC, ref.shape[-1])
+
+    def rows_of(j):
+        first = (start + j) * C
+        return select(by_dp_ref[...] + jnp.where(second, ((1 - mine) * H + j) * C, first), got1)
 
     def two(j):
-        send2[j, 0] = rows_of(start + j)
-        send2[j, 1] = rows_of((1 - mine) * H + j)
+        send2[j] = rows_of(j)
         copy(send2.at[j], rows.at[x], s2s.at[j], s2r.at[x], (start + j, d)).start()
 
     peers(H, x, two)
     cross_act.wait_recv()
     give(1)
-    rows[x, 0] = rows_of(e)
-    rows[x, 1] = rows_of(other)
+    rows[x] = rows_of(x)
 
     for i in range(2):
         peers(
@@ -126,11 +127,10 @@
         )
 
     def order(j, carry):
-        for i in range(2):
-            act_rows[j, i] = select(by_act_ref[...] + (i * N * HC + j * C), act)
+        act_rows[j] = select(by_act_ref[...] + j * C, act)
         return carry
 
-    lax.fori_loop(0, H, order, 0)
+    lax.fori_loop(0, H, order, 0, unroll=H <= 8)
     peers(
         H, x,
         lambda j: copy(send2.at[j], rows.at[j], s2s.at[j], s2r.at[j], (start + j, d)).wait_recv(),
@@ -230,8 +230,8 @@
     NC, EC, HC = N * C, E * C, H * C
     block, ff = down_weight.shape[1:]
     parts = max(1, block // 256)
-    by_dp = np.array([[j // C * EC + j % C] for j in range(NC)], np.int32)
-    by_act = np.array([[j // C * HC + j % C] for j in range(NC)], np.int32)
+    by_dp = np.array([[j // C * EC + j % C] for j in range(NC)] * 2, np.int32)
+    by_act = np.array([[i * N * HC + j // C * HC + j % C] for i in range(2) for j in range(NC)], np.int32)
     by_e = np.array(
         [[i // C % H * 2 * NC + i // HC * NC + i % C] for i in range(EC)], np.int32
     )

time: 64.5 us -> 63.7 us (0.988)
  Pallas kernels: 56.7 us -> 55.9 us
    pallas_call x1, Pallas kernels: 56.7 us -> 55.9 us  [on_device(): pl.pallas_call(functools.partial(kernel, E, N, C), out_shape=(jax.ShapeDt...]
where the time goes in v4:
time: 63.7 us; the launch traced here: 63.1 us
  Pallas kernels  55.9 us (88%)
  local copies, waits for them, and re-layouts  6.61 us (10%)
  between operations  0.65 us (1%)
    pallas_call x1, Pallas kernels, on_device(): pl.pallas_call(functools.partial(kernel, E, N, C), out_shape=(jax.ShapeDt...  55.9 us
    unnamed x11, local copies, waits for them, and re-layouts  6.61 us

profile of v4, /device:TPU:1, one launch (start us, length us, event | category | flops | bytes accessed | tf_op | source)
XLA Modules:
  0.0 63.1 jit_solution(5418485197203126035)
XLA Ops:
  0.6 0.0 copy-start.1
  0.6 0.6 %copy-done.1 = bf16[128,1]{0,1:T(2,128)(2,1)S(1)} copy-done((bf16[128,1]{0,1:T(2,128)(2,1)S(1)}, bf16[128,1]{0,1:T(2,128)(2,1)}, u32[]{:S(2)}) %copy-start.1) | copy-done | bytes 280
  1.3 0.0 copy-start.2
  1.3 0.7 %copy.11.prob_ref = bf16[128,1]{1,0:T(8,128)(2,1)} copy(bf16[128,1]{0,1:T(2,128)(2,1)S(1)} %copy-done.1) | data formatting | bytes 512 | tf_op args[1]
  2.0 0.0 copy-done.2
  2.0 0.7 %copy.12.slot_ref = s32[128,1]{1,0:T(8,128)} copy(s32[128,1]{0,1:T(1,128)S(1)} %copy-done.2) | data formatting | bytes 1024 | tf_op args[2]
  2.8 55.9 %expert_backward.1 = (f32[512,512]{1,0:T(8,128)}, bf16[192,1024]{1,0:T(8,128)(2,1)}, f32[128,1]{1,0:T(8,128)}) custom-call(bf16[128,2048]{1,0:T(8,128)(2,1)} %cot_ref.1, bf16[128,1]{1,0:T(8,128)(2,1)} %copy.11.prob_ref, s32[128,1]{1,0:T(8,128)} %copy.12.slot_ref, bf16[192,1024]{1,0:T(8,128)(2,1)} %bitcast.6, bf16[512,512]{1,0:T(8,128)(2,1)} %bitcast.5, ...), custom_call_target="tpu_custom_call" | custom-call | tf_op jit(solution)/shard_map/expert_backward/pallas_call | solution.py:240
  58.6 1.4 %copy.13 = f32[128,1]{0,1:T(1,128)} copy(f32[128,1]{1,0:T(8,128)} %get-tuple-element.11) | data formatting | bytes 1024
  60.1 0.0 copy-start
  60.1 2.3 %copy.16 = f32[1,512,512]{2,1,0:T(8,128)} copy(f32[1,512,512]{2,1,0:T(8,128)} %bitcast.4) | data formatting | bytes 2097152
  62.4 0.0 copy-done
  62.4 0.7 %copy.17 = bf16[1,192,1024]{2,1,0:T(8,128)(2,1)} copy(bf16[1,192,1024]{2,1,0:T(8,128)(2,1)S(1)} %bitcast.7) | data formatting | bytes 786432
Async XLA Ops:
  0.6 0.7 %copy-start.1 = (bf16[128,1]{0,1:T(2,128)(2,1)S(1)}, bf16[128,1]{0,1:T(2,128)(2,1)}, u32[]{:S(2)}) copy-start(bf16[128,1]{0,1:T(2,128)(2,1)} %param.9) | copy-start | bytes 772
  1.3 0.7 %copy-start.2 = (s32[128,1]{0,1:T(1,128)S(1)}, s32[128,1]{0,1:T(1,128)}, u32[]{:S(2)}) copy-start(s32[128,1]{0,1:T(1,128)} %param.10) | copy-start | bytes 1540
  60.1 2.3 %copy-start = (bf16[192,1024]{1,0:T(8,128)(2,1)S(1)}, bf16[192,1024]{1,0:T(8,128)(2,1)}, u32[]{:S(2)}) copy-start(bf16[192,1024]{1,0:T(8,128)(2,1)} %get-tuple-element.7) | copy-start | bytes 1179652

commit v5 on v3

--- a/solution.py
+++ b/solution.py
@@ -39,7 +39,7 @@
             body(lax.rem(me + k, n))
             return carry
 
-        lax.fori_loop(1, n, step, 0)
+        lax.fori_loop(1, n, step, 0, unroll=n <= 8)
 
     barrier = pltpu.get_barrier_semaphore()
     peers(N, d, lambda j: pl.semaphore_signal(barrier, inc=1, device_id=(e, j), device_id_type=MESH))
@@ -101,14 +101,17 @@
         peers(N, d, lambda j: copy(act.at[i, d], act.at[i, d], as_.at[i, j], ar.at[i, d], (e, j)).start())
 
     give(0)
-    lane_r = lax.broadcasted_iota(jnp.int32, (NC, N * EC), 1)
+    lane_r = lax.broadcasted_iota(jnp.int32, (2 * NC, N * EC), 1)
+    second = lax.broadcasted_iota(jnp.int32, (2 * NC, 1), 0) >= NC
 
     def select(base, ref):
         pick = jnp.where(lane_r == base, 1.0, 0.0).astype(BF16)
-        return jnp.dot(pick, ref.reshape(N * EC, ref.shape[-1]), preferred_element_type=F32).astype(BF16)
-
-    def rows_of(s, c):
-        return select(by_dp_ref[...] + s * C, got1[c])
+        picked = jnp.dot(pick, ref.reshape(N * EC, ref.shape[-1]), preferred_element_type=F32).astype(BF16)
+        return picked.reshape(2, NC, ref.shape[-1])
+
+    def rows_of(j, c):
+        first = (start + j) * C
+        return select(by_dp_ref[...] + jnp.where(second, ((1 - mine) * H + j) * C, first), got1[c])
 
     for c in range(parts):
         peers(
@@ -119,15 +122,13 @@
         )
 
         def two(j):
-            send2[c, j, 0] = rows_of(start + j, c)
-            send2[c, j, 1] = rows_of((1 - mine) * H + j, c)
+            send2[c, j] = rows_of(j, c)
             copy(
                 send2.at[c, j], rows.at[c, x], s2s.at[c, j], s2r.at[c, x], (start + j, d)
             ).start()
 
         peers(H, x, two)
-        rows[c, x, 0] = rows_of(e, c)
-        rows[c, x, 1] = rows_of(other, c)
+        rows[c, x] = rows_of(x, c)
         if c == 0:
             cross_act.wait_recv()
             give(1)
@@ -139,11 +140,10 @@
         )
 
     def order(j, carry):
-        for i in range(2):
-            act_rows[j, i] = select(by_act_ref[...] + (i * N * HC + j * C), act[...])
+        act_rows[j] = select(by_act_ref[...] + j * C, act[...])
         return carry
 
-    lax.fori_loop(0, H, order, 0)
+    lax.fori_loop(0, H, order, 0, unroll=H <= 8)
     lined = act_rows[...].reshape(E * NC, ff)
     for c in range(parts):
         peers(
@@ -251,8 +251,8 @@
     NC, EC, HC = N * C, E * C, H * C
     block, ff = down_weight.shape[1:]
     parts = max(1, block // 256)
-    by_dp = np.array([[j // C * EC + j % C] for j in range(NC)], np.int32)
-    by_act = np.array([[j // C * HC + j % C] for j in range(NC)], np.int32)
+    by_dp = np.array([[j // C * EC + j % C] for j in range(NC)] * 2, np.int32)
+    by_act = np.array([[i * N * HC + j // C * HC + j % C] for i in range(2) for j in range(NC)], np.int32)
     by_e = np.array(
         [[i // C % H * 2 * NC + i // HC * NC + i % C] for i in range(EC)], np.int32
     )

time: 65.8 us -> 64.8 us (0.985)
  Pallas kernels: 58 us -> 57 us
    pallas_call x1, Pallas kernels: 58 us -> 57 us  [on_device(): pl.pallas_call(functools.partial(kernel, E, N, C), out_shape=(jax.ShapeDt...]
where the time goes in v5:
time: 64.8 us; the launch traced here: 64.2 us
  Pallas kernels  57 us (88%)
  local copies, waits for them, and re-layouts  6.61 us (10%)
  between operations  0.65 us (1%)
    pallas_call x1, Pallas kernels, on_device(): pl.pallas_call(functools.partial(kernel, E, N, C), out_shape=(jax.ShapeDt...  57 us
    unnamed x11, local copies, waits for them, and re-layouts  6.61 us

profile of v5, /device:TPU:1, one launch (start us, length us, event | category | flops | bytes accessed | tf_op | source)
XLA Modules:
  0.0 64.2 jit_solution(8552713207016017306)
XLA Ops:
  0.6 0.0 copy-start.1
  0.6 0.6 %copy-done.1 = bf16[128,1]{0,1:T(2,128)(2,1)S(1)} copy-done((bf16[128,1]{0,1:T(2,128)(2,1)S(1)}, bf16[128,1]{0,1:T(2,128)(2,1)}, u32[]{:S(2)}) %copy-start.1) | copy-done | bytes 280
  1.3 0.0 copy-start.2
  1.3 0.7 %copy.11.prob_ref = bf16[128,1]{1,0:T(8,128)(2,1)} copy(bf16[128,1]{0,1:T(2,128)(2,1)S(1)} %copy-done.1) | data formatting | bytes 512 | tf_op args[1]
  2.0 0.0 copy-done.2
  2.0 0.7 %copy.12.slot_ref = s32[128,1]{1,0:T(8,128)} copy(s32[128,1]{0,1:T(1,128)S(1)} %copy-done.2) | data formatting | bytes 1024 | tf_op args[2]
  2.8 57.0 %expert_backward.1 = (f32[512,512]{1,0:T(8,128)}, bf16[192,1024]{1,0:T(8,128)(2,1)}, f32[128,1]{1,0:T(8,128)}) custom-call(bf16[128,2048]{1,0:T(8,128)(2,1)} %cot_ref.1, bf16[128,1]{1,0:T(8,128)(2,1)} %copy.11.prob_ref, s32[128,1]{1,0:T(8,128)} %copy.12.slot_ref, bf16[192,1024]{1,0:T(8,128)(2,1)} %bitcast.6, bf16[512,512]{1,0:T(8,128)(2,1)} %bitcast.5, ...), custom_call_target="tpu_custom_call" | custom-call | tf_op jit(solution)/shard_map/expert_backward/pallas_call | solution.py:261
  59.7 1.4 %copy.13 = f32[128,1]{0,1:T(1,128)} copy(f32[128,1]{1,0:T(8,128)} %get-tuple-element.11) | data formatting | bytes 1024
  61.2 0.0 copy-start
  61.2 2.3 %copy.16 = f32[1,512,512]{2,1,0:T(8,128)} copy(f32[1,512,512]{2,1,0:T(8,128)} %bitcast.4) | data formatting | bytes 2097152
  63.5 0.0 copy-done
  63.5 0.7 %copy.17 = bf16[1,192,1024]{2,1,0:T(8,128)(2,1)} copy(bf16[1,192,1024]{2,1,0:T(8,128)(2,1)S(1)} %bitcast.7) | data formatting | bytes 786432
Async XLA Ops:
  0.6 0.7 %copy-start.1 = (bf16[128,1]{0,1:T(2,128)(2,1)S(1)}, bf16[128,1]{0,1:T(2,128)(2,1)}, u32[]{:S(2)}) copy-start(bf16[128,1]{0,1:T(2,128)(2,1)} %param.9) | copy-start | bytes 772
  1.3 0.7 %copy-start.2 = (s32[128,1]{0,1:T(1,128)S(1)}, s32[128,1]{0,1:T(1,128)}, u32[]{:S(2)}) copy-start(s32[128,1]{0,1:T(1,128)} %param.10) | copy-start | bytes 1540
  61.2 2.3 %copy-start = (bf16[192,1024]{1,0:T(8,128)(2,1)S(1)}, bf16[192,1024]{1,0:T(8,128)(2,1)}, u32[]{:S(2)}) copy-start(bf16[192,1024]{1,0:T(8,128)(2,1)} %get-tuple-element.7) | copy-start | bytes 1179652
